TPU v7x, 32 devices: a whole 2x2x4 slice. The times are simulated.
32 devices in a mesh: chan: 8 (over z, x), tile: 4 (over y, core).
Axes of the slice: x: 2, y: 2, z: 4, core: 2. Of those that a mesh axis runs over, the one named last changes fastest.
Arguments:
- gamma_pair: bfloat16 [8, 2048, 2048], P('chan', 'tile'), may hold values from -8 to 8, as said below
- energies: float32 [8, 2048], P('chan'), may hold values from 0.5 to 4
- occupancy: int32 [8, 2048], P('chan'), may hold values from 0 to 2
- recoup: bfloat16 [8, 128, 128], replicated, may hold values from -0.5 to 0.5
- recoup_class: int32 [8, 16, 16], P('chan', 'tile'), may hold values from 0 to 7
- send_slot: int32 [8, 16, 16], P('chan', 'tile'), may hold values from 0 to 63, as said below
- recv_slot: int32 [8, 16, 16], P('chan', 'tile'), may hold values from 0 to 63, as said below
Outputs:
- flowed: float32 [8, 2048, 2048], P('chan', 'tile')
Inputs may be any that keep to these rules, and one draw needn't show every extreme that they name: gamma_pair is symmetric in its last two dimensions. `send_slot`: for each channel and block b, the 64 entries of tile rows b * 4 to (b + 1) * 4 - 1 are a permutation of 0 to 63; entry q = 8 * c + s with 0 <= s < 8 sends the tile to channel c in its slot s, so each channel receives exactly 8 tiles from each block of each channel. `recv_slot`: for each channel and block b, the 64 entries of tile rows b * 4 to (b + 1) * 4 - 1 are a permutation of 0 to 63; entry q = 8 * c + s with 0 <= s < 8 names the tile received from channel c in its slot s.
All inputs are finite; a program needn't handle non-finite values.
Results may differ from a plain program's by a relative error of at most 0.002.
Values may be sent and summed in bfloat16 or wider, within the bound.
A program may use at most 128 MiB of HBM per device.

v0:
```python
import math

import jax
import jax.numpy as jnp
from jax import lax
from jax.sharding import PartitionSpec as P


def split_tiles(matrix, tile_size):
    row_count = matrix.shape[1]
    full_width = matrix.shape[2]
    blocks = matrix.reshape(row_count // tile_size, tile_size, full_width // tile_size, tile_size)
    return jnp.transpose(blocks, (0, 2, 1, 3)).reshape(-1, tile_size, tile_size)


def join_tiles(tile_set, row_count, full_width):
    tile_size = tile_set.shape[1]
    blocks = tile_set.reshape(row_count // tile_size, full_width // tile_size, tile_size, tile_size)
    return jnp.transpose(blocks, (0, 2, 1, 3)).reshape(1, row_count, full_width)


def on_device(gamma_pair, energies, occupancy, recoup, recoup_class, send_slot, recv_slot):
    row_count = gamma_pair.shape[1]
    full_width = gamma_pair.shape[2]
    tile_size = recoup.shape[1]
    first_row = lax.axis_index("tile") * row_count
    occ_float = occupancy[0].astype(jnp.float32)
    energy_all = energies[0]
    occ_rows = lax.dynamic_slice_in_dim(occ_float, first_row, row_count)
    energy_rows = lax.dynamic_slice_in_dim(energy_all, first_row, row_count)
    upper_mask = ((occ_rows[:, None] == 0.0) & (occ_float[None, :] == 2.0)).astype(jnp.float32)
    lower_mask = ((occ_rows[:, None] == 2.0) & (occ_float[None, :] == 0.0)).astype(jnp.float32)
    denom = energy_rows[:, None] + energy_all[None, :]
    eta_local = (gamma_pair[0].astype(jnp.float32) * (upper_mask - lower_mask) / denom).astype(
        jnp.bfloat16
    )[None]
    weight_p = (1.0 - occ_float).astype(jnp.bfloat16)
    eta_scaled = eta_local * weight_p[None, None, :]
    columns = eta_scaled
    ladder_half = jnp.einsum(
        "crk,ckn->crn",
        columns,
        lax.all_gather(gamma_pair, "tile", axis=1, tiled=True),
        preferred_element_type=jnp.float32,
    )
    gamma_scaled = gamma_pair * weight_p[None, None, :]
    ladder_mirror = jnp.einsum(
        "crk,cnk->crn",
        gamma_scaled,
        lax.all_gather(eta_local, "tile", axis=1, tiled=True),
        preferred_element_type=jnp.float32,
    )
    ladder = ladder_half + ladder_mirror
    class_flat = recoup_class.reshape(-1)
    picker = (class_flat[:, None] == jnp.arange(recoup.shape[0], dtype=jnp.int32)[None, :]).astype(
        jnp.bfloat16
    )
    chosen = jnp.dot(
        picker, recoup.reshape(recoup.shape[0], -1), preferred_element_type=jnp.float32
    )
    chosen = chosen.astype(jnp.bfloat16).reshape(-1, tile_size, tile_size)

    def recouple(matrix):
        return jnp.einsum(
            "kab,kbd->kad",
            split_tiles(matrix, tile_size),
            chosen,
            preferred_element_type=jnp.float32,
        ).astype(jnp.bfloat16)

    send_flat = send_slot.reshape(-1)
    recv_flat = recv_slot.reshape(-1)
    send_sorter = jnp.argsort(send_flat)
    eta_out = recouple(eta_local)[send_sorter]
    gamma_out = recouple(gamma_pair)[send_sorter]
    eta_in, gamma_in = (
        lax.all_to_all(eta_out, "chan", split_axis=0, concat_axis=0, tiled=True),
        lax.all_to_all(gamma_out, "chan", split_axis=0, concat_axis=0, tiled=True),
    )
    eta_cross = join_tiles(eta_in[recv_flat], row_count, full_width)
    gamma_cross = join_tiles(gamma_in[recv_flat], row_count, full_width)
    eta_whole = lax.all_gather(eta_cross, "tile", axis=1, tiled=True)
    shard_rows = lax.all_gather(gamma_cross, "tile", axis=1, tiled=True)
    own_columns = lax.dynamic_slice_in_dim(shard_rows, first_row, row_count, 2)
    mirror_part = jnp.einsum(
        "ckr,cnk->crn", own_columns, eta_whole, preferred_element_type=jnp.float32
    )
    columns = eta_cross
    cross_half = jnp.einsum("crk,ckn->crn", columns, shard_rows, preferred_element_type=jnp.float32)
    cross_sym = (cross_half - mirror_part).astype(jnp.bfloat16)
    recv_sorter = jnp.argsort(recv_flat)
    returned = lax.all_to_all(
        split_tiles(cross_sym, tile_size)[recv_sorter],
        "chan",
        split_axis=0,
        concat_axis=0,
        tiled=True,
    )
    pair_tiles = returned[send_flat]
    back_tiles = jnp.einsum("kab,kdb->kad", pair_tiles, chosen, preferred_element_type=jnp.float32)
    back_full = join_tiles(back_tiles, row_count, full_width)
    step_size = 1.0 / math.sqrt(full_width)
    return gamma_pair.astype(jnp.float32) + step_size * (ladder + back_full)


def solution(mesh):
    placed = (
        P("chan", "tile", None),
        P("chan", None),
        P("chan", None),
        P(),
        P("chan", "tile", None),
        P("chan", "tile", None),
        P("chan", "tile", None),
    )
    return jax.shard_map(
        on_device, mesh=mesh, in_specs=placed, out_specs=P("chan", "tile", None), check_vma=False
    )
```

profile of v0, /device:TPU:0, one launch (start us, length us, event | category | flops | bytes accessed | tf_op | source)
XLA Modules:
  0.0 367.3 jit_solution(11587672603299470363)
XLA Ops:
  6.5 3.6 copy.20
  10.1 0.1 eq.61
  10.2 0.7 fusion.30
  11.0 0.6 copy.22
  11.6 0.1 copy-done.5
  11.7 0.1 reshape.392
  11.7 0.1 reshape.405
  11.8 2.1 sort.31
  13.9 2.1 sort.32
  16.1 2.0 bitcast_bitcast_fusion
  18.0 0.5 copy.14
  18.6 3.0 convert_bitcast_fusion
  21.6 3.7 %gather_fusion.2 = bf16[64,128,128]{1,2,0:T(8,128)(2,1)} fusion(bf16[64,128,128]{1,2,0:T(8,128)(2,1)} %convert_bitcast_fusion, s32[1024]{0:T(1024)S(1)} %pad_clamp_fusion.3), kind=kCustom, calls=%fused_computation.2 | custom fusion | bytes 4194560 | tf_op jit(solution)/shard_map/gather | solution.py:75
  25.3 7.2 %all-to-all-start.1 = ((bf16[64,128,128]{1,2,0:T(8,128)(2,1)}), bf16[64,128,128]{1,2,0:T(8,128)(2,1)}, u32[]{:S(2)}, u32[]{:S(2)}) async-start(bf16[64,128,128]{1,2,0:T(8,128)(2,1)} %gather_fusion.2), calls=%async_computation.1 | async-start | bytes 4194304 | tf_op jit(solution)/shard_map/all_to_all | solution.py:78
  32.5 0.1 reshape.393
  32.6 48.2 %all-to-all-done.1 = bf16[64,128,128]{1,2,0:T(8,128)(2,1)} async-done(((bf16[64,128,128]{1,2,0:T(8,128)(2,1)}), bf16[64,128,128]{1,2,0:T(8,128)(2,1)}, u32[]{:S(2)}, u32[]{:S(2)}) %all-to-all-start.1) | async-done | bytes 2097184 | tf_op jit(solution)/shard_map/all_to_all | solution.py:78
  80.8 3.7 %gather_fusion.3 = bf16[64,128,128]{1,2,0:T(8,128)(2,1)} fusion(bf16[64,128,128]{1,2,0:T(8,128)(2,1)} %all-to-all-done.1, s32[1024]{0:T(1024)S(1)} %pad_clamp_fusion.2), kind=kCustom, calls=%fused_computation.3 | custom fusion | bytes 4194560 | tf_op jit(solution)/shard_map/gather | solution.py:81
  84.5 4.5 %copy.16 = bf16[4,16,128,128]{3,1,2,0:T(8,128)(2,1)} copy(bf16[4,16,128,128]{2,3,1,0:T(8,128)(2,1)} %bitcast.121) | data formatting | bytes 4194304 | tf_op jit(solution)/shard_map/reshape | solution.py:18
  89.0 4.2 %reshape.398 = bf16[1,512,2048]{2,1,0:T(8,128)(2,1)} reshape(bf16[4,128,16,128]{3,2,1,0:T(8,128)(2,1)} %bitcast.122) | data formatting | bytes 4194304 | tf_op jit(solution)/shard_map/reshape | solution.py:19
  93.3 0.6 copy-done.2
  94.0 0.1 compare_reduce_fusion.1
  94.0 5.6 %fusion.16 = bf16[4,16,128,128]{3,1,2,0:T(8,128)(2,1)S(1)} fusion(f32[16,128]{1,0:T(8,128)S(1)} %bitcast.126, f32[4,128]{1,0:T(4,128)S(1)} %bitcast.129, pred[16,128]{1,0:T(8,128)(4,1)S(1)} %bitcast.133, pred[4,128]{1,0:T(4,128)(4,1)S(1)} %bitcast.135, pred[16,128]{1,0:T(8,128)(4,1)S(1)} %bitcast.132, pred[4,128]{1,0:T(4,128)(4,1)S(1)} %bitcast.134, ...), kind=kLoop, calls=%fused_computation.24 | loop fusion | flops 10485760 | bytes 4209664 | tf_op jit(solution)/shard_map/transpose | solution.py:13
  99.7 0.5 copy.12
  100.2 2.0 convolution_convert_fusion.1
  102.2 4.2 %gather_fusion = bf16[64,128,128]{2,1,0:T(8,128)(2,1)} fusion(bf16[64,128,128]{2,1,0:T(8,128)(2,1)} %convolution_convert_fusion.1, s32[1024]{0:T(1024)S(1)} %pad_clamp_fusion.3), kind=kCustom, calls=%fused_computation | custom fusion | bytes 4194560 | tf_op jit(solution)/shard_map/gather | solution.py:74
  106.5 52.1 %all_to_all.15 = bf16[64,128,128]{2,1,0:T(8,128)(2,1)} all-to-all(bf16[64,128,128]{2,1,0:T(8,128)(2,1)} %gather_fusion), channel_id=1, replica_groups=mesh['chan'=8,'tile'=4] {'chan'}, dimensions={0} | all-to-all | bytes 4194304 | tf_op jit(solution)/shard_map/all_to_all | solution.py:77
  158.6 3.7 %gather_fusion.1 = bf16[64,128,128]{2,1,0:T(8,128)(2,1)} fusion(bf16[64,128,128]{2,1,0:T(8,128)(2,1)} %all_to_all.15, s32[1024]{0:T(1024)S(1)} %pad_clamp_fusion.2), kind=kCustom, calls=%fused_computation.1 | custom fusion | bytes 4194560 | tf_op jit(solution)/shard_map/gather | solution.py:80
  162.3 4.2 %copy.37 = bf16[4,16,128,128]{3,1,2,0:T(8,128)(2,1)} copy(bf16[4,16,128,128]{3,2,1,0:T(8,128)(2,1)} %bitcast.119) | data formatting | bytes 4194304 | tf_op jit(solution)/shard_map/reshape | solution.py:18
  166.6 4.2 %reshape.401 = bf16[1,512,2048]{2,1,0:T(8,128)(2,1)} reshape(bf16[4,128,16,128]{3,2,1,0:T(8,128)(2,1)} %bitcast.117) | data formatting | bytes 4194304 | tf_op jit(solution)/shard_map/reshape | solution.py:19
  170.8 4.3 %fusion.9 = bf16[1,512,2048]{2,1,0:T(8,128)(2,1)} fusion(bf16[1,512,2048]{2,1,0:T(8,128)(2,1)} %param.7, f32[2048]{0:T(1024)S(1)} %bitcast.127, f32[512]{0:T(512)S(1)} %bitcast.130, pred[2048]{0:T(1024)(128)(4,1)S(1)} %get-tuple-element.12, pred[2048]{0:T(1024)(128)(4,1)S(1)} %get-tuple-element.11, pred[512]{0:T(512)(128)(4,1)S(1)} %get-tuple-element.10, ...), kind=kLoop, calls=%fused_computation.18 | loop fusion | flops 10485760 | bytes 4209664 | tf_op jit(solution)/shard_map/convert_element_type | solution.py:34
  175.1 0.2 all-gather.5.cloned.1.call-start
  175.3 0.3 all-gather.5.cloned.1.call-update
  175.7 11.9 %fusion.2 = f32[512,2048]{1,0:T(8,128)} fusion(bf16[1,2048,2048]{2,1,0:T(8,128)(2,1)} %all-gather.9.cloned.1.call-done, bf16[64,8,16,128]{3,2,1,0:T(8,128)(2,1)} %bitcast.118), kind=kOutput, calls=%fused_computation.9 | convolution fusion | flops 4294967296 | bytes 14680064 | tf_op jit(solution)/shard_map/crk,ckn->crn/dot_general | solution.py:89
  187.7 40.5 %all-gather.11.cloned.1.call-done = bf16[1,2048,2048]{2,1,0:T(8,128)(2,1)} async-done(((bf16[1,512,2048]{2,1,0:T(8,128)(2,1)}), bf16[1,2048,2048]{2,1,0:T(8,128)(2,1)}) %all-gather.11.cloned.1.call-update) | async-done | bytes 8388624 | tf_op jit(solution)/shard_map/all_gather | solution.py:82
  228.2 9.7 %fusion.25 = bf16[64,8,16,128]{3,1,2,0:T(8,128)(2,1)S(1)} fusion(f32[512,2048]{1,0:T(8,128)} %fusion.2, bf16[1,2048,2048]{2,1,0:T(8,128)(2,1)} %all-gather.11.cloned.1.call-done, bf16[1,2048,2048]{2,1,0:T(8,128)(2,1)} %all-gather.9.cloned.1.call-done, s32[]{:T(128)S(6)} %select_n.33), kind=kOutput, calls=%fused_computation.36 | convolution fusion | flops 4297064448 | bytes 16777220 | tf_op jit(solution)/shard_map/ckr,cnk->crn/dot_general | solution.py:85
  237.9 0.6 copy.24
  238.6 1.9 copy.17
  240.4 4.2 %gather_fusion.4 = bf16[64,128,128]{2,1,0:T(8,128)(2,1)} fusion(bf16[64,128,128]{2,1,0:T(8,128)(2,1)} %bitcast.120, s32[1024]{0:T(1024)S(1)} %pad_clamp_fusion.1), kind=kCustom, calls=%fused_computation.4 | custom fusion | bytes 4194560 | tf_op jit(solution)/shard_map/gather | solution.py:93
  244.6 5.6 %all-to-all-start.2 = ((bf16[64,128,128]{2,1,0:T(8,128)(2,1)}), bf16[64,128,128]{2,1,0:T(8,128)(2,1)}, u32[]{:S(2)}, u32[]{:S(2)}) async-start(bf16[64,128,128]{2,1,0:T(8,128)(2,1)} %gather_fusion.4), calls=%async_computation.2 | async-start | bytes 4194304 | tf_op jit(solution)/shard_map/all_to_all | solution.py:92
  250.3 0.1 reshape.406
  250.4 37.7 %all-gather.7.cloned.1.call-done = bf16[1,2048,2048]{2,1,0:T(8,128)(2,1)} async-done(((bf16[1,512,2048]{2,1,0:T(8,128)(2,1)}), bf16[1,2048,2048]{2,1,0:T(8,128)(2,1)}) %all-gather.7.cloned.1.call-update) | async-done | bytes 8388624 | tf_op jit(solution)/shard_map/all_gather | solution.py:50
  288.1 10.7 %fusion.4 = f32[512,2048]{1,0:T(8,128)} fusion(bf16[1,2048,2048]{2,1,0:T(8,128)(2,1)} %all-gather.7.cloned.1.call-done, bf16[1,512,2048]{2,1,0:T(8,128)(2,1)} %param.7, bf16[2048]{0:T(1024)(128)(2,1)S(1)} %convert_reduce_fusion), kind=kOutput, calls=%fused_computation.11 | convolution fusion | flops 4296015872 | bytes 14684160 | tf_op jit(solution)/shard_map/crk,cnk->crn/dot_general | solution.py:47
  298.7 0.3 all-to-all-done.2
  299.0 4.0 %gather_fusion.5 = bf16[64,128,128]{2,1,0:T(8,128)(2,1)} fusion(bf16[64,128,128]{2,1,0:T(8,128)(2,1)} %all-to-all-done.2, s32[1024]{0:T(1024)S(1)} %pad_clamp_fusion), kind=kCustom, calls=%fused_computation.5 | custom fusion | bytes 4194560 | tf_op jit(solution)/shard_map/gather | solution.py:99
  303.0 3.2 fusion.40
  306.2 4.4 %copy.18 = f32[4,16,128,128]{3,1,2,0:T(8,128)} copy(f32[4,16,128,128]{3,2,1,0:T(8,128)S(1)} %bitcast.114) | data formatting | bytes 8388608 | tf_op jit(solution)/shard_map/reshape | solution.py:18
  310.6 37.2 %all-gather.5.cloned.1.call-done = bf16[1,2048,2048]{2,1,0:T(8,128)(2,1)} async-done(((bf16[1,512,2048]{2,1,0:T(8,128)(2,1)}), bf16[1,2048,2048]{2,1,0:T(8,128)(2,1)}) %all-gather.5.cloned.1.call-update) | async-done | bytes 8388624 | tf_op jit(solution)/shard_map/all_gather | solution.py:43
  347.8 13.0 %convert_add_fusion = f32[1,512,2048]{2,1,0:T(8,128)} fusion(bf16[1,512,2048]{2,1,0:T(8,128)(2,1)S(1)} %copy-done, f32[64,8,16,128]{3,2,1,0:T(8,128)} %bitcast.124, f32[512,2048]{1,0:T(8,128)} %fusion.4, bf16[1,2048,2048]{2,1,0:T(8,128)(2,1)} %all-gather.5.cloned.1.call-done, bf16[2048]{0:T(1024)(128)(2,1)S(1)} %convert_reduce_fusion, ...), kind=kOutput, calls=%fused_computation.15 | convolution fusion | flops 4314890240 | bytes 23088128 | tf_op jit(solution)/shard_map/crk,ckn->crn/dot_general | solution.py:40
  (32 shorter events, 0.4 us)
Async XLA Ops:
  6.5 3.6 copy-start.6
  6.5 3.7 %copy-start.1 = (bf16[8,128,128]{2,1,0:T(8,128)(2,1)S(1)}, bf16[8,128,128]{2,1,0:T(8,128)(2,1)}, u32[]{:S(2)}) copy-start(bf16[8,128,128]{2,1,0:T(8,128)(2,1)} %param.10) | copy-start | bytes 786436
  11.0 0.7 copy-start.5
  11.0 0.8 copy-start.4
  25.3 55.6 %all-to-all-start.1 = ((bf16[64,128,128]{1,2,0:T(8,128)(2,1)}), bf16[64,128,128]{1,2,0:T(8,128)(2,1)}, u32[]{:S(2)}, u32[]{:S(2)}) async-start(bf16[64,128,128]{1,2,0:T(8,128)(2,1)} %gather_fusion.2), calls=%async_computation.1 | async-start | bytes 4194304 | tf_op jit(solution)/shard_map/all_to_all | solution.py:78
  32.5 143.2 %all-gather.9.cloned.1.call-start = ((), (), s32[]{:S(2)}) async-start(), calls=%async_computation.5 | async-start | bytes 10485760 | tf_op jit(solution)/shard_map/all_gather | solution.py:83
  93.2 0.7 copy-start.2
  93.2 0.7 copy-start.3
  93.2 135.0 %all-gather.11.cloned.1.call-start = ((), (), s32[]{:S(2)}) async-start(), calls=%async_computation.6 | async-start | bytes 10485760 | tf_op jit(solution)/shard_map/all_gather | solution.py:82
  170.8 117.3 %all-gather.7.cloned.1.call-start = ((), (), s32[]{:S(2)}) async-start(), calls=%async_computation.4 | async-start | bytes 10485760 | tf_op jit(solution)/shard_map/all_gather | solution.py:50
  175.1 172.7 %all-gather.5.cloned.1.call-start = ((), (), s32[]{:S(2)}) async-start(), calls=%async_computation.3 | async-start | bytes 10485760 | tf_op jit(solution)/shard_map/all_gather | solution.py:43
  244.6 54.4 %all-to-all-start.2 = ((bf16[64,128,128]{2,1,0:T(8,128)(2,1)}), bf16[64,128,128]{2,1,0:T(8,128)(2,1)}, u32[]{:S(2)}, u32[]{:S(2)}) async-start(bf16[64,128,128]{2,1,0:T(8,128)(2,1)} %gather_fusion.4), calls=%async_computation.2 | async-start | bytes 4194304 | tf_op jit(solution)/shard_map/all_to_all | solution.py:92
  306.2 41.7 %copy-start = (bf16[1,512,2048]{2,1,0:T(8,128)(2,1)S(1)}, bf16[1,512,2048]{2,1,0:T(8,128)(2,1)}, u32[]{:S(2)}) copy-start(bf16[1,512,2048]{2,1,0:T(8,128)(2,1)} %param.7) | copy-start | bytes 6291460
Sparse Core Ops, SparseCore 0:
  93.4 57.3 all-gather.8
  170.9 57.2 all-gather.10
  229.8 58.2 all-gather.6
  289.5 58.2 all-gather.4
where the time goes:
time: 368 us; the launch traced here: 367 us
  waiting for transfers between devices  164 us (45%)
  local copies, waits for them, and re-layouts  55.9 us (15%)
  matrix products  54.2 us (15%)
  blocking collectives  52.1 us (14%)
  other arithmetic  14.3 us (4%)
  between operations  13.3 us (4%)
  starting transfers between devices  13.2 us (4%)
    all_to_all x1, blocking collectives, on_device(): lax.all_to_all(eta_out, 'chan', split_axis=0, concat_axis=0, tiled=True)  52.1 us
    all_to_all x1, waiting for transfers between devices, on_device(): lax.all_to_all(gamma_out, 'chan', split_axis=0, concat_axis=0, tiled=True)  48.2 us
    all_gather x1, waiting for transfers between devices, on_device(): eta_whole = lax.all_gather(eta_cross, 'tile', axis=1, tiled=True)  40.5 us
    all_gather x1, waiting for transfers between devices, on_device(): lax.all_gather(eta_local, 'tile', axis=1, tiled=True)  37.7 us
    all_gather x1, waiting for transfers between devices, on_device(): lax.all_gather(gamma_pair, 'tile', axis=1, tiled=True)  37.2 us
    reshape x3, local copies, waits for them, and re-layouts, join_tiles(): tile_set.reshape(row_count // tile_size, full_width // tile_size, tile_si...  13.2 us
    dot_general x1, matrix products, on_device(): jnp.einsum('crk,ckn->crn', columns, lax.all_gather(gamma_pair, 'tile', ax...  13 us
    dot_general x1, matrix products, on_device(): jnp.einsum('crk,ckn->crn', columns, shard_rows, preferred_element_type=jn...  11.9 us
  transfers between devices with their start and end apart: 6, of which 5 were waited for; matrix products, arithmetic and copies ran while one was open for 22% of the time, Pallas kernels for 0%

commit v1 on v0

v1 whole, which is shorter than its diff:
```python
import functools
import math

import jax
import jax.numpy as jnp
from jax import lax
from jax.experimental import pallas as pl
from jax.experimental.pallas import tpu as pltpu
from jax.sharding import PartitionSpec as P

MIB = 1024 * 1024
VMEM = pltpu.VMEM
SMEM = pltpu.SMEM


def whole(memory=VMEM):
    return pl.BlockSpec(memory_space=memory)


def sort_kernel(cols, tile, slot_ref, x_ref, out_ref):
    i = pl.program_id(0)
    for j in range(cols):
        out_ref[slot_ref[i * cols + j]] = x_ref[:, j * tile : (j + 1) * tile]


def sort_tiles(matrix, slots, tile):
    rows, width = matrix.shape
    cols = width // tile
    count = (rows // tile) * cols
    return pl.pallas_call(
        functools.partial(sort_kernel, cols, tile),
        grid=(rows // tile,),
        in_specs=[whole(SMEM), pl.BlockSpec((tile, width), lambda i: (i, 0))],
        out_specs=pl.BlockSpec((count, tile, tile), lambda i: (0, 0, 0)),
        out_shape=jax.ShapeDtypeStruct((count, tile, tile), matrix.dtype),
        compiler_params=pltpu.CompilerParams(vmem_limit_bytes=24 * MIB),
        name="sort_tiles",
    )(slots, matrix)


def ladder_kernel(block, row_count, where_ref, gamma_ref, xrow_ref, xcol_ref, out_ref, left):
    width = gamma_ref.shape[0]
    first = pl.multiple_of(where_ref[0], row_count)

    def scaled(g, a, b):
        return jnp.where(a * b < 0.0, -g.astype(jnp.float32) / jnp.abs(a - b), 0.0).astype(jnp.bfloat16)

    @pl.when(pl.program_id(0) == 0)
    def _():
        for i in range(row_count // 128):
            rows = pl.ds(first + i * 128, 128)
            left[i * 128 : (i + 1) * 128, :] = scaled(gamma_ref[rows, :], xrow_ref[rows, :], xcol_ref[...])

    cols = pl.ds(pl.multiple_of(pl.program_id(0) * block, block), block)
    right = gamma_ref[:, cols]
    total = jnp.dot(left[...], right, preferred_element_type=jnp.float32)
    eta = scaled(right, xrow_ref[...], xcol_ref[:, cols])
    total += jnp.dot(gamma_ref[pl.ds(first, row_count), :], eta, preferred_element_type=jnp.float32)
    out_ref[...] = total


def ladder_product(gamma_full, x, first, row_count):
    width = gamma_full.shape[0]
    block = 256
    return pl.pallas_call(
        functools.partial(ladder_kernel, block, row_count),
        grid=(width // block,),
        in_specs=[whole(SMEM), whole(), whole(), whole()],
        out_specs=pl.BlockSpec((row_count, block), lambda j: (0, j)),
        out_shape=jax.ShapeDtypeStruct((row_count, width), jnp.float32),
        scratch_shapes=[VMEM((row_count, width), jnp.bfloat16)],
        compiler_params=pltpu.CompilerParams(vmem_limit_bytes=48 * MIB),
        cost_estimate=pl.CostEstimate(
            flops=4 * row_count * width * width, bytes_accessed=8 * width * width, transcendentals=0
        ),
        name="ladder",
    )(first, gamma_full, x[:, None], x[None, :])


def cross_kernel(
    grid_cols, block, row_count, per_block, where_ref, recv_ref, meta_ref, raw_ref, recoup_ref, xseg_ref, xturn_ref, out_ref,
    eta_s, gamma_s,
):
    tile = recoup_ref.shape[1]
    lane = lax.broadcasted_iota(jnp.int32, (tile, 128), 1)
    slots = meta_ref.shape[0] // raw_ref.shape[0]
    first = pl.multiple_of(where_ref[0], row_count)
    tile_rows = per_block // grid_cols

    def place(n):
        b = n // per_block
        p = lax.rem(n, per_block)
        q = recv_ref[n]
        m = meta_ref[b * per_block + q]
        k = lax.rem(m, per_block)
        kind = lax.rem(m // per_block, recoup_ref.shape[0])
        source = m // (per_block * recoup_ref.shape[0])
        a_seg = source * grid_cols + b * tile_rows + k // grid_cols
        b_seg = source * grid_cols + lax.rem(k, grid_cols)
        turned = xturn_ref[a_seg // 128]
        xa = jnp.sum(jnp.where(lane == lax.rem(a_seg, 128), turned, 0.0), axis=1, keepdims=True)
        xb = xseg_ref[pl.ds(b_seg, 1), :]
        g = raw_ref[b, q]
        eta = jnp.where(xa * xb < 0.0, g.astype(jnp.float32) / (xa - xb), 0.0).astype(jnp.bfloat16)
        both = jnp.dot(jnp.concatenate([eta, g], axis=0), recoup_ref[kind], preferred_element_type=jnp.float32)
        both = both.astype(jnp.bfloat16)
        rows = pl.ds(pl.multiple_of((n // grid_cols) * tile, tile), tile)
        cols = pl.ds(pl.multiple_of(lax.rem(n, grid_cols) * tile, tile), tile)
        eta_s[rows, cols] = both[:tile]
        gamma_s[rows, cols] = both[tile:]

    def some(n, carry):
        for u in range(4):
            place(n * 4 + u)
        return carry

    lax.fori_loop(0, raw_ref.shape[0] * per_block // 4, some, 0)

    own_rows = pl.ds(first, row_count)
    me = first // row_count

    def product(jj, carry):
        cols = pl.ds(pl.multiple_of(jj * block, block), block)
        half = jnp.dot(eta_s[own_rows, :], gamma_s[:, cols], preferred_element_type=jnp.float32)
        mirror = jnp.dot(eta_s[cols, :], gamma_s[:, own_rows], preferred_element_type=jnp.float32)
        sym = (half - mirror.T).astype(jnp.bfloat16)
        for i in range(row_count // tile):
            for j in range(block // tile):
                slot = recv_ref[me * per_block + i * grid_cols + jj * (block // tile) + j]
                out_ref[slot] = sym[i * tile : (i + 1) * tile, j * tile : (j + 1) * tile]
        return carry

    lax.fori_loop(0, eta_s.shape[0] // block, product, 0)


def cross_product(raw, recoup, xseg, xturn, first, recv_all, meta, row_count):
    blocks, per_block, tile, _ = raw.shape
    width = blocks * row_count
    return pl.pallas_call(
        functools.partial(cross_kernel, width // tile, 256, row_count, per_block),
        in_specs=[whole(SMEM), whole(SMEM), whole(SMEM), whole(), whole(), whole(), whole()],
        out_specs=whole(),
        out_shape=jax.ShapeDtypeStruct((per_block, tile, tile), jnp.bfloat16),
        scratch_shapes=[VMEM((width, width), jnp.bfloat16), VMEM((width, width), jnp.bfloat16)],
        compiler_params=pltpu.CompilerParams(vmem_limit_bytes=52 * MIB),
        name="cross",
    )(first, recv_all, meta, raw, recoup, xseg, xturn)


def back_kernel(cols, step_size, slot_ref, kind_ref, tiles_ref, recoup_ref, gamma_ref, ladder_ref, out_ref):
    i = pl.program_id(0)
    tile = recoup_ref.shape[1]
    for j in range(cols):
        part = pl.ds(j * tile, tile)
        back = lax.dot_general(
            tiles_ref[slot_ref[i * cols + j]],
            recoup_ref[kind_ref[i * cols + j]],
            (((1,), (1,)), ((), ())),
            preferred_element_type=jnp.float32,
        )
        out_ref[:, part] = gamma_ref[:, part].astype(jnp.float32) + step_size * (ladder_ref[:, part] + back)


def finish(returned, recoup, gamma, ladder, slots, kinds):
    rows, width = gamma.shape
    count, tile, _ = returned.shape
    row_block = pl.BlockSpec((tile, width), lambda i: (i, 0))
    return pl.pallas_call(
        functools.partial(back_kernel, width // tile, 1.0 / math.sqrt(width)),
        grid=(rows // tile,),
        in_specs=[whole(SMEM), whole(SMEM), whole(), whole(), row_block, row_block],
        out_specs=row_block,
        out_shape=jax.ShapeDtypeStruct((rows, width), jnp.float32),
        compiler_params=pltpu.CompilerParams(vmem_limit_bytes=32 * MIB),
        name="finish",
    )(slots, kinds, returned, recoup, gamma, ladder)


def on_device(n_chan, n_tile, gamma_pair, energies, occupancy, recoup, recoup_class, send_slot, recv_slot):
    gamma = gamma_pair[0]
    row_count, width = gamma.shape
    tile = recoup.shape[1]
    tiles = (row_count // tile) * (width // tile)
    group = tiles // n_chan
    chan = lax.axis_index("chan")
    first = lax.axis_index("tile") * row_count
    send = send_slot.reshape(-1)
    recv = recv_slot.reshape(-1)
    kinds = recoup_class.reshape(-1)
    x = energies[0] * (1.0 - occupancy[0].astype(jnp.float32))

    local = jnp.arange(tiles, dtype=jnp.int32)
    hit = send[None, :] == local[:, None]
    entry = jnp.sum(jnp.where(hit, (local + tiles * kinds)[None, :], 0), axis=1)
    packed = jnp.concatenate(
        [
            lax.dynamic_slice_in_dim(x, first, row_count),
            entry.astype(jnp.float32),
            recv.astype(jnp.float32),
        ]
    )
    known = lax.all_gather(packed, ("chan", "tile"), axis=0, tiled=False).reshape(n_chan, n_tile, -1)
    x_all = known[:, :, :row_count].reshape(-1, tile)
    segments = x_all.shape[0]
    padded = jnp.pad(x_all, ((0, -segments % 128), (0, 0)))
    x_turned = jnp.swapaxes(padded.reshape(-1, 128, tile), 1, 2)
    entries = lax.dynamic_slice_in_dim(known, row_count + chan * group, group, 2).astype(jnp.int32)
    source = jnp.arange(n_chan, dtype=jnp.int32)[:, None, None]
    meta = jnp.transpose(entries + source * (tiles * recoup.shape[0]), (1, 0, 2)).reshape(-1)
    recv_all = lax.dynamic_slice_in_dim(known, chan, 1, 0)[0, :, row_count + tiles :].astype(jnp.int32).reshape(-1)
    where = first.reshape(1)

    out_tiles = sort_tiles(gamma, send, tile)
    arrived = lax.all_to_all(out_tiles, "chan", split_axis=0, concat_axis=0, tiled=True)
    raw = lax.all_gather(arrived, "tile", axis=0, tiled=False)
    gamma_full = lax.all_gather(gamma, "tile", axis=0, tiled=True)
    ladder = ladder_product(gamma_full, x, where, row_count)
    sym_tiles = cross_product(raw, recoup, padded, x_turned, where, recv_all, meta, row_count)
    returned = lax.all_to_all(sym_tiles, "chan", split_axis=0, concat_axis=0, tiled=True)
    return finish(returned, recoup, gamma, ladder, send, kinds)[None]


def solution(mesh):
    placed = (
        P("chan", "tile", None),
        P("chan", None),
        P("chan", None),
        P(),
        P("chan", "tile", None),
        P("chan", "tile", None),
        P("chan", "tile", None),
    )
    return jax.shard_map(
        functools.partial(on_device, mesh.shape["chan"], mesh.shape["tile"]),
        mesh=mesh, in_specs=placed, out_specs=P("chan", "tile", None), check_vma=False,
    )
```

time: 368 us -> 231 us (0.63)
  waiting for transfers between devices: 164 us -> 44.9 us
  Pallas kernels: 0 us -> 63.3 us
  matrix products: 54.2 us -> 0 us
  local copies, waits for them, and re-layouts: 55.9 us -> 7.47 us
  blocking collectives: 52.1 us -> 95.8 us
  other arithmetic: 14.3 us -> 0.57 us
  starting transfers between devices: 13.2 us -> 5.47 us
    all_gather x4 -> x2, waiting for transfers between devices: 115 us -> 30.5 us  [the longest x1 15.7 us: on_device(): raw = lax.all_gather(arrived, 'tile', axis=0, tiled=False)]
    pallas_call x0 -> x4, Pallas kernels: none -> 63.3 us  [the longest x1 39.2 us: cross_product(): pl.pallas_call(functools.partial(cross_kernel, width // tile, 256, row_co...]
    dot_general x8 -> x0, matrix products: 54.2 us -> none  [the longest x1 13 us: on_device(): jnp.einsum('crk,ckn->crn', columns, lax.all_gather(gamma_pair, 'tile', ax...]
    all_gather x0 -> x1, blocking collectives: none -> 40.5 us  [on_device(): lax.all_gather(packed, ('chan', 'tile'), axis=0, tiled=False)]
    all_to_all x2 -> x1, waiting for transfers between devices: 48.5 us -> 13.6 us  [on_device(): lax.all_to_all(sym_tiles, 'chan', split_axis=0, concat_axis=0, tiled=True)]
    gather x6 -> x0, local copies, waits for them, and re-layouts: 23.5 us -> none  [the longest x1 4.23 us: on_device(): eta_out = recouple(eta_local)[send_sorter]]
    reshape x10 -> x7, local copies, waits for them, and re-layouts: 23.7 us -> 1.1 us  [the longest x1 0.76 us: on_device(): send = send_slot.reshape(-1)]
    all_to_all x2 -> x1, starting transfers between devices: 12.9 us -> 5.43 us  [on_device(): lax.all_to_all(sym_tiles, 'chan', split_axis=0, concat_axis=0, tiled=True)]
  transfers between devices with their start and end apart: 6 -> 3, of which waited for: 5 -> 3; matrix products, arithmetic and copies ran while one was open for 22% -> 1% of each run, Pallas kernels for 0% -> 25%
where the time goes in v1:
time: 231 us
  blocking collectives  95.8 us (41%)
  Pallas kernels  63.3 us (27%)
  waiting for transfers between devices  44.9 us (19%)
  between operations  13.6 us (6%)
  local copies, waits for them, and re-layouts  7.47 us (3%)
  starting transfers between devices  5.47 us (2%)
    all_to_all x1, blocking collectives, on_device(): lax.all_to_all(out_tiles, 'chan', split_axis=0, concat_axis=0, tiled=True)  55.4 us
    all_gather x1, blocking collectives, on_device(): lax.all_gather(packed, ('chan', 'tile'), axis=0, tiled=False)  40.5 us
    pallas_call x1, Pallas kernels, cross_product(): pl.pallas_call(functools.partial(cross_kernel, width // tile, 256, row_co...  39.2 us
    pallas_call x1, Pallas kernels, ladder_product(): pl.pallas_call(functools.partial(ladder_kernel, block, row_count), grid=(...  18.1 us
    all_gather x1, waiting for transfers between devices, on_device(): raw = lax.all_gather(arrived, 'tile', axis=0, tiled=False)  15.7 us
    all_gather x1, waiting for transfers between devices, on_device(): gamma_full = lax.all_gather(gamma, 'tile', axis=0, tiled=True)  14.9 us
    all_to_all x1, waiting for transfers between devices, on_device(): lax.all_to_all(sym_tiles, 'chan', split_axis=0, concat_axis=0, tiled=True)  13.6 us
    unnamed x19, local copies, waits for them, and re-layouts  5.82 us
  transfers between devices with their start and end apart: 3, of which 3 were waited for; matrix products, arithmetic and copies ran while one was open for 1% of the time, Pallas kernels for 25%

profile of v1, /device:TPU:0, one launch (start us, length us, event | category | flops | bytes accessed | tf_op | source)
XLA Modules:
  0.0 231.1 jit_solution(15376542354454481846)
XLA Ops:
  6.5 0.0 all-gather.7.cloned.1.call-start
  6.5 0.8 reshape.74.slot_ref
  7.3 0.0 copy-start
  7.3 1.6 copy-done
  8.9 1.0 sort_tiles.1
  9.9 55.4 %all_to_all.10 = bf16[64,128,128]{2,1,0:T(8,128)(2,1)} all-to-all(bf16[64,128,128]{2,1,0:T(8,128)(2,1)S(1)} %sort_tiles.1), channel_id=1, replica_groups=mesh['chan'=8,'tile'=4] {'chan'}, dimensions={0} | all-to-all | bytes 4194304 | tf_op jit(solution)/shard_map/all_to_all | solution.py:214
  65.3 0.0 copy-start.7
  65.3 0.0 copy-start.8
  65.3 0.0 copy-start.5
  65.3 0.0 copy-start.6
  65.3 0.0 all-gather.7.cloned.1.call-update
  65.3 0.0 copy-start.4
  65.3 0.0 all-gather.9.cloned.1.call-start
  65.4 0.7 all-gather.9.cloned.1.call-update
  66.1 0.0 copy-done.7
  66.1 0.1 reshape.75.kind_ref
  66.2 0.1 select_reduce_fusion
  66.3 0.0 copy-done.8
  66.4 0.1 convert_element_type.35
  66.4 0.0 copy-done.5
  66.4 0.0 copy-done.6
  66.5 0.1 pad_maximum_fusion
  66.6 40.5 %all-gather.3 = f32[32,1,640]{2,1,0:T(1,128)S(1)} all-gather(f32[1,1,640]{2,1,0:T(1,128)S(1)} %reshape.85), channel_id=2, replica_groups=mesh['chan'=8,'tile'=4] {'chan','tile'}, dimensions={0}, use_global_device_ids=true | all-gather | bytes 84480 | tf_op jit(solution)/shard_map/all_gather | solution.py:202
  107.0 0.2 reduce
  107.3 0.1 dynamic-slice_convert_fusion
  107.4 0.1 convert_element_type.37.recv_ref
  107.5 0.1 add_bitcast_fusion
  107.6 0.1 reshape.78.meta_ref
  107.7 0.1 copy.15
  107.8 15.7 %all-gather.7.cloned.1.call-done = bf16[256,128,128]{2,1,0:T(8,128)(2,1)} async-done(((bf16[64,128,128]{2,1,0:T(8,128)(2,1)}), bf16[256,128,128]{2,1,0:T(8,128)(2,1)}) %all-gather.7.cloned.1.call-update) | async-done | bytes 8388624 | tf_op jit(solution)/shard_map/all_gather | solution.py:215
  123.5 0.0 copy-done.4
  123.5 39.2 %cross.1 = bf16[64,128,128]{2,1,0:T(8,128)(2,1)} custom-call(s32[1]{0:T(128)} %bitcast.where_ref, s32[256]{0:T(256)S(1)} %convert_element_type.37.recv_ref, s32[256]{0:T(256)S(1)} %reshape.78.meta_ref, bf16[4,64,128,128]{3,2,1,0:T(8,128)(2,1)} %bitcast.14, bf16[8,128,128]{2,1,0:T(8,128)(2,1)S(1)} %copy-done.4, f32[128,128]{1,0:T(8,128)S(1)} %reshape.79.xseg_ref, ...), custom_call_target="tpu_custom_call" | custom-call | tf_op jit(solution)/shard_map/cross/pallas_call | solution.py:139
  162.6 5.4 %all-to-all-start.1 = ((bf16[64,128,128]{2,1,0:T(8,128)(2,1)}), bf16[64,128,128]{2,1,0:T(8,128)(2,1)}, u32[]{:S(2)}, u32[]{:S(2)}) async-start(bf16[64,128,128]{2,1,0:T(8,128)(2,1)} %cross.1), calls=%async_computation.1 | async-start | bytes 4194304 | tf_op jit(solution)/shard_map/all_to_all | solution.py:219
  168.1 0.4 copy.16.xrow_ref
  168.4 14.9 %all-gather.9.cloned.1.call-done = bf16[1,2048,2048]{2,1,0:T(8,128)(2,1)} async-done(((bf16[1,512,2048]{2,1,0:T(8,128)(2,1)}), bf16[1,2048,2048]{2,1,0:T(8,128)(2,1)}) %all-gather.9.cloned.1.call-update) | async-done | bytes 8388624 | tf_op jit(solution)/shard_map/all_gather | solution.py:216
  183.3 0.0 copy-start.1
  183.3 18.1 %ladder.1.ladder_ref = f32[512,2048]{1,0:T(8,128)S(1)} custom-call(s32[1]{0:T(128)} %bitcast.where_ref, bf16[2048,2048]{1,0:T(8,128)(2,1)} %bitcast.16, f32[2048,1]{1,0:T(8,128)S(1)} %copy.16.xrow_ref, f32[1,2048]{1,0:T(1,128)S(1)} %subtract_multiply_fusion.xcol_ref), custom_call_target="tpu_custom_call" | custom-call | flops 8589934592 | bytes 33554432 | tf_op jit(solution)/shard_map/ladder/pallas_call | solution.py:65
  201.4 0.0 copy-start.2
  201.4 2.0 copy-done.2
  203.4 13.6 %all-to-all-done.1.tiles_ref = bf16[64,128,128]{2,1,0:T(8,128)(2,1)} async-done(((bf16[64,128,128]{2,1,0:T(8,128)(2,1)}), bf16[64,128,128]{2,1,0:T(8,128)(2,1)}, u32[]{:S(2)}, u32[]{:S(2)}) %all-to-all-start.1) | async-done | bytes 2097184 | tf_op jit(solution)/shard_map/all_to_all | solution.py:219
  217.0 0.0 copy-done.1
  217.0 0.0 copy-start.3
  217.0 2.2 copy-done.3
  219.2 5.1 %finish.1 = f32[512,2048]{1,0:T(8,128)} custom-call(s32[64]{0:T(128)S(1)} %reshape.74.slot_ref, s32[64]{0:T(128)S(1)} %reshape.75.kind_ref, bf16[64,128,128]{2,1,0:T(8,128)(2,1)} %all-to-all-done.1.tiles_ref, bf16[8,128,128]{2,1,0:T(8,128)(2,1)S(1)} %copy-done.4, bf16[512,2048]{1,0:T(8,128)(2,1)S(1)} %bitcast.11, f32[512,2048]{1,0:T(8,128)S(1)} %copy-done.3), custom_call_target="tpu_custom_call" | custom-call | tf_op jit(solution)/shard_map/finish/pallas_call | solution.py:168
  (12 shorter events, 0.1 us)
Async XLA Ops:
  6.5 116.9 %all-gather.7.cloned.1.call-start = ((), (), s32[]{:S(2)}) async-start(), calls=%async_computation.2 | async-start | bytes 10485760 | tf_op jit(solution)/shard_map/all_gather | solution.py:215
  7.3 1.6 copy-start
  65.3 0.8 copy-start.7
  65.3 1.0 copy-start.8
  65.3 1.1 copy-start.5
  65.3 1.1 copy-start.6
  65.3 58.1 %copy-start.4 = (bf16[8,128,128]{2,1,0:T(8,128)(2,1)S(1)}, bf16[8,128,128]{2,1,0:T(8,128)(2,1)}, u32[]{:S(2)}) copy-start(bf16[8,128,128]{2,1,0:T(8,128)(2,1)} %recoup_ref.3) | copy-start | bytes 786436
  65.3 118.0 %all-gather.9.cloned.1.call-start = ((), (), s32[]{:S(2)}) async-start(), calls=%async_computation.3 | async-start | bytes 10485760 | tf_op jit(solution)/shard_map/all_gather | solution.py:216
  162.6 54.4 %all-to-all-start.1 = ((bf16[64,128,128]{2,1,0:T(8,128)(2,1)}), bf16[64,128,128]{2,1,0:T(8,128)(2,1)}, u32[]{:S(2)}, u32[]{:S(2)}) async-start(bf16[64,128,128]{2,1,0:T(8,128)(2,1)} %cross.1), calls=%async_computation.1 | async-start | bytes 4194304 | tf_op jit(solution)/shard_map/all_to_all | solution.py:219
  183.3 33.7 %copy-start.1 = (bf16[1,512,2048]{2,1,0:T(8,128)(2,1)S(1)}, bf16[1,512,2048]{2,1,0:T(8,128)(2,1)}, u32[]{:S(2)}) copy-start(bf16[1,512,2048]{2,1,0:T(8,128)(2,1)} %param.7) | copy-start | bytes 6291460
  201.4 2.0 copy-start.2
  217.0 2.2 copy-start.3
Sparse Core Ops, SparseCore 0:
  65.5 57.9 all-gather.6
  125.0 58.2 all-gather.8

commit v2 on v1

--- a/solution.py
+++ b/solution.py
@@ -38,43 +38,186 @@
     )(slots, matrix)
 
 
-def ladder_kernel(block, row_count, where_ref, gamma_ref, xrow_ref, xcol_ref, out_ref, left):
-    width = gamma_ref.shape[0]
-    first = pl.multiple_of(where_ref[0], row_count)
+def exchange_kernel(
+    n_chan, block, group, sorted_ref, gamma_ref, info_ref, xrow_ref, xcol_ref, raw_ref, known_ref, ladder_ref,
+    full, left, a_send, a_recv, f_send, f_recv, g_send, g_recv, l_sem,
+):
+    chan = lax.axis_index("chan")
+    t = lax.axis_index("tile")
+    near = t + 1 - 2 * lax.rem(t, 2)
+    far = lax.rem(t + 2, 4)
+    row_count, width = gamma_ref.shape
+    half = width // 2
+    steps = width // block
+
+    barrier = pltpu.get_barrier_semaphore()
+    for k in range(1, n_chan):
+        pl.semaphore_signal(
+            barrier, inc=1, device_id=(lax.rem(chan + k, n_chan), t), device_id_type=pl.DeviceIdType.MESH
+        )
+    for peer in (near, far):
+        pl.semaphore_signal(barrier, inc=1, device_id=(chan, peer), device_id_type=pl.DeviceIdType.MESH)
+    pl.semaphore_wait(barrier, n_chan + 1)
+
+    def remote(src, dst, send, recv, device):
+        return pltpu.make_async_remote_copy(
+            src_ref=src, dst_ref=dst, send_sem=send, recv_sem=recv, device_id=device, device_id_type=pl.DeviceIdType.MESH
+        )
+
+    def tiles_of(c):
+        return pl.ds(c * group, group)
+
+    def outgoing(k):
+        to = lax.rem(chan + k, n_chan)
+        return (
+            remote(info_ref, known_ref.at[chan, t], a_send.at[1, k], a_recv.at[1, k], (to, t)),
+            remote(sorted_ref.at[tiles_of(to)], raw_ref.at[t, tiles_of(chan)], a_send.at[0, k], a_recv.at[0, k], (to, t)),
+        )
+
+    def onward(kind, k):
+        source = lax.rem(chan - k + n_chan, n_chan)
+        b = far if kind == 2 else t
+        device = (chan, far if kind == 0 else near)
+        at = raw_ref.at[b, tiles_of(source)]
+        info = known_ref.at[source, b]
+        return (
+            remote(info, info, f_send.at[1, kind, k], f_recv.at[1, kind, k], device),
+            remote(at, at, f_send.at[0, kind, k], f_recv.at[0, kind, k], device),
+        )
+
+    def each(copies, what):
+        for copy in copies:
+            getattr(copy, what)()
+
+    rows = pl.ds(t * row_count, row_count)
+    far_rows = pl.ds(far * row_count, row_count)
+    own_half = pl.multiple_of((t // 2) * half, half)
+    far_half = pl.multiple_of(half - own_half, half)
+    own_cols = pl.ds(own_half, half)
+    far_cols = pl.ds(far_half, half)
+    over = remote(gamma_ref.at[:, own_cols], full.at[rows, own_cols], g_send.at[0], g_recv.at[0], (chan, far))
+    beside = remote(gamma_ref, full.at[rows, :], g_send.at[1], g_recv.at[1], (chan, near))
+    passed = remote(full.at[far_rows, far_cols], full.at[far_rows, far_cols], g_send.at[2], g_recv.at[2], (chan, near))
+    mine = pltpu.make_async_copy(sorted_ref.at[tiles_of(chan)], raw_ref.at[t, tiles_of(chan)], l_sem.at[0])
+    mine_info = pltpu.make_async_copy(info_ref, known_ref.at[chan, t], l_sem.at[1])
+
+    over.start()
+    beside.start()
+    mine.start()
+    mine_info.start()
+
+    def send_out(k, carry):
+        each(outgoing(k), "start")
+        return carry
+
+    lax.fori_loop(1, n_chan, send_out, 0)
+    full[rows, :] = gamma_ref[...]
+    mine.wait()
+    mine_info.wait()
+    each(onward(0, 0), "start")
+    each(onward(1, 0), "start")
 
     def scaled(g, a, b):
         return jnp.where(a * b < 0.0, -g.astype(jnp.float32) / jnp.abs(a - b), 0.0).astype(jnp.bfloat16)
 
-    @pl.when(pl.program_id(0) == 0)
-    def _():
-        for i in range(row_count // 128):
-            rows = pl.ds(first + i * 128, 128)
-            left[i * 128 : (i + 1) * 128, :] = scaled(gamma_ref[rows, :], xrow_ref[rows, :], xcol_ref[...])
-
-    cols = pl.ds(pl.multiple_of(pl.program_id(0) * block, block), block)
-    right = gamma_ref[:, cols]
-    total = jnp.dot(left[...], right, preferred_element_type=jnp.float32)
-    eta = scaled(right, xrow_ref[...], xcol_ref[:, cols])
-    total += jnp.dot(gamma_ref[pl.ds(first, row_count), :], eta, preferred_element_type=jnp.float32)
-    out_ref[...] = total
-
-
-def ladder_product(gamma_full, x, first, row_count):
-    width = gamma_full.shape[0]
-    block = 256
+    for i in range(row_count // 128):
+        part = slice(i * 128, (i + 1) * 128)
+        own = pl.ds(pl.multiple_of(t * row_count + i * 128, 128), 128)
+        left[part, :] = scaled(gamma_ref[part, :], xrow_ref[own, :], xcol_ref[...])
+
+    over.wait_recv()
+    passed.start()
+    beside.wait_recv()
+    passed.wait_recv()
+
+    def turn(n, carry):
+        across = pl.multiple_of(lax.rem(n, half // 256) * 256, 256)
+        down = pl.multiple_of((n // (half // 256)) * 256, 256)
+        piece = full[pl.ds(own_half + down, 256), pl.ds(far_half + across, 256)]
+        full[pl.ds(far_half + across, 256), pl.ds(own_half + down, 256)] = piece.T
+        return carry
+
+    passed.wait_send()
+    lax.fori_loop(0, (half // 256) ** 2, turn, 0)
+
+    def ladder_block(j):
+        cols = pl.ds(pl.multiple_of(j * block, block), block)
+        right = full[:, cols]
+        total = jnp.dot(left[...], right, preferred_element_type=jnp.float32)
+        eta = scaled(right, xrow_ref[...], xcol_ref[:, cols])
+        ladder_ref[:, cols] = total + jnp.dot(gamma_ref[...], eta, preferred_element_type=jnp.float32)
+
+    def step(k, carry):
+        each(outgoing(k), "wait_recv")
+        each(onward(0, k), "start")
+        each(onward(1, k), "start")
+        each(onward(0, k - 1), "wait_recv")
+        each(onward(2, k - 1), "start")
+
+        @pl.when(k <= steps)
+        def _():
+            ladder_block(k - 1)
+
+        return carry
+
+    lax.fori_loop(1, n_chan, step, 0)
+    each(onward(0, n_chan - 1), "wait_recv")
+    each(onward(2, n_chan - 1), "start")
+
+    def rest(j, carry):
+        ladder_block(j)
+        return carry
+
+    lax.fori_loop(min(n_chan - 1, steps), steps, rest, 0)
+
+    def drain(k, carry):
+        each(onward(1, k), "wait_recv")
+        each(onward(2, k), "wait_recv")
+        for kind in range(3):
+            each(onward(kind, k), "wait_send")
+        return carry
+
+    def drain_out(k, carry):
+        each(outgoing(k), "wait_send")
+        return carry
+
+    lax.fori_loop(0, n_chan, drain, 0)
+    lax.fori_loop(1, n_chan, drain_out, 0)
+    over.wait_send()
+    beside.wait_send()
+
+
+def exchange(sorted_tiles, gamma, info, x, n_chan, n_tile):
+    rows, width = gamma.shape
+    count, tile, _ = sorted_tiles.shape
+    anywhere = whole(pl.ANY)
+    dma = pltpu.SemaphoreType.DMA
     return pl.pallas_call(
-        functools.partial(ladder_kernel, block, row_count),
-        grid=(width // block,),
-        in_specs=[whole(SMEM), whole(), whole(), whole()],
-        out_specs=pl.BlockSpec((row_count, block), lambda j: (0, j)),
-        out_shape=jax.ShapeDtypeStruct((row_count, width), jnp.float32),
-        scratch_shapes=[VMEM((row_count, width), jnp.bfloat16)],
-        compiler_params=pltpu.CompilerParams(vmem_limit_bytes=48 * MIB),
+        functools.partial(exchange_kernel, n_chan, 256, count // n_chan),
+        in_specs=[anywhere, whole(), anywhere, whole(), whole()],
+        out_specs=[anywhere, anywhere, whole()],
+        out_shape=[
+            jax.ShapeDtypeStruct((n_tile, count, tile, tile), gamma.dtype),
+            jax.ShapeDtypeStruct((n_chan, n_tile) + info.shape, info.dtype),
+            jax.ShapeDtypeStruct((rows, width), jnp.float32),
+        ],
+        scratch_shapes=[
+            VMEM((width, width), jnp.bfloat16),
+            VMEM((rows, width), jnp.bfloat16),
+            dma((2, n_chan)),
+            dma((2, n_chan)),
+            dma((2, 3, n_chan)),
+            dma((2, 3, n_chan)),
+            dma((3,)),
+            dma((3,)),
+            dma((2,)),
+        ],
+        compiler_params=pltpu.CompilerParams(vmem_limit_bytes=48 * MIB, collective_id=0, has_side_effects=True),
         cost_estimate=pl.CostEstimate(
-            flops=4 * row_count * width * width, bytes_accessed=8 * width * width, transcendentals=0
+            flops=4 * rows * width * width, bytes_accessed=16 * width * width, transcendentals=0
         ),
-        name="ladder",
-    )(first, gamma_full, x[:, None], x[None, :])
+        name="exchange",
+    )(sorted_tiles, gamma, info, x[:, None], x[None, :])
 
 
 def cross_kernel(
@@ -199,7 +342,11 @@
             recv.astype(jnp.float32),
         ]
     )
-    known = lax.all_gather(packed, ("chan", "tile"), axis=0, tiled=False).reshape(n_chan, n_tile, -1)
+    length = packed.shape[0]
+    info = jnp.pad(packed, (0, -length % (8 * 128))).reshape(-1, 128)
+    out_tiles = sort_tiles(gamma, send, tile)
+    raw, known, ladder = exchange(out_tiles, gamma, info, x, n_chan, n_tile)
+    known = known.reshape(n_chan, n_tile, -1)[:, :, :length]
     x_all = known[:, :, :row_count].reshape(-1, tile)
     segments = x_all.shape[0]
     padded = jnp.pad(x_all, ((0, -segments % 128), (0, 0)))
@@ -210,11 +357,6 @@
     recv_all = lax.dynamic_slice_in_dim(known, chan, 1, 0)[0, :, row_count + tiles :].astype(jnp.int32).reshape(-1)
     where = first.reshape(1)
 
-    out_tiles = sort_tiles(gamma, send, tile)
-    arrived = lax.all_to_all(out_tiles, "chan", split_axis=0, concat_axis=0, tiled=True)
-    raw = lax.all_gather(arrived, "tile", axis=0, tiled=False)
-    gamma_full = lax.all_gather(gamma, "tile", axis=0, tiled=True)
-    ladder = ladder_product(gamma_full, x, where, row_count)
     sym_tiles = cross_product(raw, recoup, padded, x_turned, where, recv_all, meta, row_count)
     returned = lax.all_to_all(sym_tiles, "chan", split_axis=0, concat_axis=0, tiled=True)
     return finish(returned, recoup, gamma, ladder, send, kinds)[None]

time: 231 us -> 189 us (0.82)
  Pallas kernels: 63.3 us -> 126 us
  waiting for transfers between devices: 44.9 us -> 0 us
  blocking collectives: 95.8 us -> 52.8 us
  between operations: 13.6 us -> 0.14 us
  starting transfers between devices: 5.47 us -> 0 us
    pallas_call x1, Pallas kernels: 18.1 us -> 82.1 us  [exchange(): pl.pallas_call(functools.partial(exchange_kernel, n_chan, 256, count // n...]
    all_gather x1 -> x0, blocking collectives: 40.5 us -> none  [on_device(): lax.all_gather(packed, ('chan', 'tile'), axis=0, tiled=False)]
    all_gather x2 -> x0, waiting for transfers between devices: 30.5 us -> none  [the longest x1 15.7 us: on_device(): raw = lax.all_gather(arrived, 'tile', axis=0, tiled=False)]
    all_to_all x1 -> x0, waiting for transfers between devices: 13.6 us -> none  [on_device(): lax.all_to_all(sym_tiles, 'chan', split_axis=0, concat_axis=0, tiled=True)]
    all_to_all x1 -> x0, starting transfers between devices: 5.43 us -> none  [on_device(): lax.all_to_all(sym_tiles, 'chan', split_axis=0, concat_axis=0, tiled=True)]
    all_to_all x1, blocking collectives: 55.4 us -> 52.8 us  [on_device(): lax.all_to_all(sym_tiles, 'chan', split_axis=0, concat_axis=0, tiled=True)]
    unnamed x19 -> x16, local copies, waits for them, and re-layouts: 5.82 us -> 4.52 us
  transfers between devices with their start and end apart: 3 -> 0, of which waited for: 3 -> 0; matrix products, arithmetic and copies ran while one was open for 1% -> 0% of each run, Pallas kernels for 25% -> 0%
where the time goes in v2:
time: 189 us; the launch traced here: 188 us
  Pallas kernels  126 us (67%)
  blocking collectives  52.8 us (28%)
  local copies, waits for them, and re-layouts  6.89 us (4%)
  other arithmetic  2.23 us (1%)
    pallas_call x1, Pallas kernels, exchange(): pl.pallas_call(functools.partial(exchange_kernel, n_chan, 256, count // n...  82.1 us
    all_to_all x1, blocking collectives, on_device(): lax.all_to_all(sym_tiles, 'chan', split_axis=0, concat_axis=0, tiled=True)  52.8 us
    pallas_call x1, Pallas kernels, cross_product(): pl.pallas_call(functools.partial(cross_kernel, width // tile, 256, row_co...  39.1 us
    unnamed x16, local copies, waits for them, and re-layouts  4.52 us
    pallas_call x1, Pallas kernels, finish(): pl.pallas_call(functools.partial(back_kernel, width // tile, 1.0 / math.s...  4.04 us

profile of v2, /device:TPU:0, one launch (start us, length us, event | category | flops | bytes accessed | tf_op | source)
XLA Modules:
  0.0 188.3 jit_solution(1907760830419415181)
XLA Ops:
  0.0 0.5 iota_multiply_fusion
  0.5 0.8 reshape.77.slot_ref
  1.3 0.8 reshape.78.kind_ref
  2.1 0.1 select_reduce_fusion
  2.2 0.7 convert_element_type.36
  2.9 0.1 convert_element_type.37
  3.0 0.0 copy-start
  3.0 1.6 copy-done
  4.6 0.0 copy-start.6
  4.6 0.0 copy-start.7
  4.6 0.0 copy-start.1
  4.6 1.0 sort_tiles.1.sorted_ref
  5.6 0.0 copy-start.3
  5.6 1.3 copy-done.3
  6.9 0.0 copy-done.6
  6.9 0.0 copy-done.7
  6.9 0.4 copy.11.xrow_ref
  7.3 0.1 fusion.info_ref
  7.4 0.0 copy-done.1
  7.4 0.0 copy-start.4
  7.4 1.6 copy-done.4
  9.0 0.0 copy-start.5
  9.0 82.1 %exchange.1 = (bf16[4,64,128,128]{3,2,1,0:T(8,128)(2,1)}, f32[8,4,8,128]{3,2,1,0:T(8,128)S(1)}, f32[512,2048]{1,0:T(8,128)}) custom-call(bf16[64,128,128]{2,1,0:T(8,128)(2,1)S(1)} %copy-done.4, bf16[512,2048]{1,0:T(8,128)(2,1)S(1)} %bitcast.13, f32[8,128]{1,0:T(8,128)S(1)} %fusion.info_ref, f32[2048,1]{1,0:T(8,128)S(1)} %copy.11.xrow_ref, ...), custom_call_target="tpu_custom_call" | custom-call | flops 8589934592 | bytes 67108864 | tf_op jit(solution)/shard_map/exchange/pallas_call | solution.py:195
  91.3 0.7 add_bitcast_fusion
  92.0 0.1 reshape.82.meta_ref
  92.1 0.1 dynamic-slice_convert_fusion
  92.2 0.1 convert_element_type.39.recv_ref
  92.3 0.1 copy.13
  92.4 0.0 copy-done.5
  92.4 39.1 %cross.1 = bf16[64,128,128]{2,1,0:T(8,128)(2,1)} custom-call(s32[1]{0:T(128)} %bitcast.where_ref, s32[256]{0:T(256)S(1)} %convert_element_type.39.recv_ref, s32[256]{0:T(256)S(1)} %reshape.82.meta_ref, bf16[4,64,128,128]{3,2,1,0:T(8,128)(2,1)} %get-tuple-element.9.raw_ref, bf16[8,128,128]{2,1,0:T(8,128)(2,1)S(1)} %copy-done.5, ...), custom_call_target="tpu_custom_call" | custom-call | tf_op jit(solution)/shard_map/cross/pallas_call | solution.py:282
  131.4 0.0 copy-start.2
  131.4 52.8 %all_to_all.5.tiles_ref = bf16[64,128,128]{2,1,0:T(8,128)(2,1)S(1)} all-to-all(bf16[64,128,128]{2,1,0:T(8,128)(2,1)} %cross.1), channel_id=1, replica_groups=mesh['chan'=8,'tile'=4] {'chan'}, dimensions={0} | all-to-all | bytes 4194304 | tf_op jit(solution)/shard_map/all_to_all | solution.py:361
  184.3 0.0 copy-done.2
  184.3 4.0 %finish.1 = f32[512,2048]{1,0:T(8,128)} custom-call(s32[64]{0:T(128)S(1)} %reshape.77.slot_ref, s32[64]{0:T(128)S(1)} %reshape.78.kind_ref, bf16[64,128,128]{2,1,0:T(8,128)(2,1)S(1)} %all_to_all.5.tiles_ref, bf16[8,128,128]{2,1,0:T(8,128)(2,1)S(1)} %copy-done.5, bf16[512,2048]{1,0:T(8,128)(2,1)S(1)} %bitcast.14, f32[512,2048]{1,0:T(8,128)S(1)} %copy-done.2), custom_call_target="tpu_custom_call" | custom-call | tf_op jit(solution)/shard_map/finish/pallas_call | solution.py:311
  (10 shorter events, 0.2 us)
Async XLA Ops:
  3.0 1.6 copy-start
  4.6 2.3 %copy-start.6 = (f32[1,2048]{1,0:T(1,128)S(1)}, f32[1,2048]{1,0:T(1,128)}, u32[]{:S(2)}) copy-start(f32[1,2048]{1,0:T(1,128)} %param.8) | copy-start | bytes 24580
  4.6 2.3 %copy-start.7 = (s32[1,2048]{1,0:T(1,128)S(1)}, s32[1,2048]{1,0:T(1,128)}, u32[]{:S(2)}) copy-start(s32[1,2048]{1,0:T(1,128)} %param.9) | copy-start | bytes 24580
  4.6 2.8 %copy-start.1 = (bf16[1,512,2048]{2,1,0:T(8,128)(2,1)S(1)}, bf16[1,512,2048]{2,1,0:T(8,128)(2,1)}, u32[]{:S(2)}) copy-start(bf16[1,512,2048]{2,1,0:T(8,128)(2,1)} %param.7) | copy-start | bytes 6291460
  5.6 1.3 copy-start.3
  7.4 1.6 copy-start.4
  9.0 83.4 %copy-start.5 = (bf16[8,128,128]{2,1,0:T(8,128)(2,1)S(1)}, bf16[8,128,128]{2,1,0:T(8,128)(2,1)}, u32[]{:S(2)}) copy-start(bf16[8,128,128]{2,1,0:T(8,128)(2,1)} %recoup_ref.3) | copy-start | bytes 786436
  131.4 52.8 %copy-start.2 = (f32[512,2048]{1,0:T(8,128)S(1)}, f32[512,2048]{1,0:T(8,128)}, u32[]{:S(2)}) copy-start(f32[512,2048]{1,0:T(8,128)} %get-tuple-element.10.ladder_ref) | copy-start | bytes 12582916

commit v3 on v2

--- a/solution.py
+++ b/solution.py
@@ -125,6 +125,16 @@
         own = pl.ds(pl.multiple_of(t * row_count + i * 128, 128), 128)
         left[part, :] = scaled(gamma_ref[part, :], xrow_ref[own, :], xcol_ref[...])
 
+    def forward(k, carry):
+        each(outgoing(k), "wait_recv")
+        each(onward(0, k), "start")
+        each(onward(1, k), "start")
+        each(onward(0, k - 1), "wait_recv")
+        each(onward(2, k - 1), "start")
+        return carry
+
+    early = n_chan // 2
+    lax.fori_loop(1, early, forward, 0)
     over.wait_recv()
     passed.start()
     beside.wait_recv()
@@ -148,27 +158,23 @@
         ladder_ref[:, cols] = total + jnp.dot(gamma_ref[...], eta, preferred_element_type=jnp.float32)
 
     def step(k, carry):
-        each(outgoing(k), "wait_recv")
-        each(onward(0, k), "start")
-        each(onward(1, k), "start")
-        each(onward(0, k - 1), "wait_recv")
-        each(onward(2, k - 1), "start")
-
-        @pl.when(k <= steps)
+        forward(k, 0)
+
+        @pl.when(k < early + steps)
         def _():
-            ladder_block(k - 1)
-
-        return carry
-
-    lax.fori_loop(1, n_chan, step, 0)
+            ladder_block(k - early)
+
+        return carry
+
+    lax.fori_loop(early, n_chan, step, 0)
+
+    def rest(j, carry):
+        ladder_block(j)
+        return carry
+
+    lax.fori_loop(min(n_chan - early, steps), steps, rest, 0)
     each(onward(0, n_chan - 1), "wait_recv")
     each(onward(2, n_chan - 1), "start")
-
-    def rest(j, carry):
-        ladder_block(j)
-        return carry
-
-    lax.fori_loop(min(n_chan - 1, steps), steps, rest, 0)
 
     def drain(k, carry):
         each(onward(1, k), "wait_recv")
@@ -253,11 +259,11 @@
         gamma_s[rows, cols] = both[tile:]
 
     def some(n, carry):
-        for u in range(4):
-            place(n * 4 + u)
-        return carry
-
-    lax.fori_loop(0, raw_ref.shape[0] * per_block // 4, some, 0)
+        for u in range(8):
+            place(n * 8 + u)
+        return carry
+
+    lax.fori_loop(0, raw_ref.shape[0] * per_block // 8, some, 0)
 
     own_rows = pl.ds(first, row_count)
     me = first // row_count

time: 189 us -> 185 us (0.979)
  Pallas kernels: 126 us -> 122 us
    pallas_call x1, Pallas kernels: 39.1 us -> 32.3 us  [cross_product(): pl.pallas_call(functools.partial(cross_kernel, width // tile, 256, row_co...]
    pallas_call x1, Pallas kernels: 82.1 us -> 84.5 us  [exchange(): pl.pallas_call(functools.partial(exchange_kernel, n_chan, 256, count // n...]
where the time goes in v3:
time: 185 us
  Pallas kernels  122 us (66%)
  blocking collectives  53.8 us (29%)
  local copies, waits for them, and re-layouts  6.89 us (4%)
  other arithmetic  2.23 us (1%)
    pallas_call x1, Pallas kernels, exchange(): pl.pallas_call(functools.partial(exchange_kernel, n_chan, 256, count // n...  84.5 us
    all_to_all x1, blocking collectives, on_device(): lax.all_to_all(sym_tiles, 'chan', split_axis=0, concat_axis=0, tiled=True)  53.8 us
    pallas_call x1, Pallas kernels, cross_product(): pl.pallas_call(functools.partial(cross_kernel, width // tile, 256, row_co...  32.3 us
    unnamed x16, local copies, waits for them, and re-layouts  4.52 us
    pallas_call x1, Pallas kernels, finish(): pl.pallas_call(functools.partial(back_kernel, width // tile, 1.0 / math.s...  4.04 us

profile of v3, /device:TPU:0, one launch (start us, length us, event | category | flops | bytes accessed | tf_op | source)
XLA Modules:
  0.0 184.8 jit_solution(10709772344082504883)
XLA Ops:
  0.0 0.5 iota_multiply_fusion
  0.5 0.8 reshape.77.slot_ref
  1.3 0.8 reshape.78.kind_ref
  2.1 0.1 select_reduce_fusion
  2.2 0.7 convert_element_type.36
  2.9 0.1 convert_element_type.37
  3.0 0.0 copy-start
  3.0 1.6 copy-done
  4.6 0.0 copy-start.6
  4.6 0.0 copy-start.7
  4.6 0.0 copy-start.1
  4.6 1.0 sort_tiles.1.sorted_ref
  5.6 0.0 copy-start.3
  5.6 1.3 copy-done.3
  6.9 0.0 copy-done.6
  6.9 0.0 copy-done.7
  6.9 0.4 copy.11.xrow_ref
  7.3 0.1 fusion.info_ref
  7.4 0.0 copy-done.1
  7.4 0.0 copy-start.4
  7.4 1.6 copy-done.4
  9.0 0.0 copy-start.5
  9.0 84.5 %exchange.1 = (bf16[4,64,128,128]{3,2,1,0:T(8,128)(2,1)}, f32[8,4,8,128]{3,2,1,0:T(8,128)S(1)}, f32[512,2048]{1,0:T(8,128)}) custom-call(bf16[64,128,128]{2,1,0:T(8,128)(2,1)S(1)} %copy-done.4, bf16[512,2048]{1,0:T(8,128)(2,1)S(1)} %bitcast.13, f32[8,128]{1,0:T(8,128)S(1)} %fusion.info_ref, f32[2048,1]{1,0:T(8,128)S(1)} %copy.11.xrow_ref, ...), custom_call_target="tpu_custom_call" | custom-call | flops 8589934592 | bytes 67108864 | tf_op jit(solution)/shard_map/exchange/pallas_call | solution.py:201
  93.7 0.7 add_bitcast_fusion
  94.4 0.1 reshape.82.meta_ref
  94.5 0.1 dynamic-slice_convert_fusion
  94.5 0.1 convert_element_type.39.recv_ref
  94.6 0.1 copy.13
  94.7 0.0 copy-done.5
  94.7 32.3 %cross.1 = bf16[64,128,128]{2,1,0:T(8,128)(2,1)} custom-call(s32[1]{0:T(128)} %bitcast.where_ref, s32[256]{0:T(256)S(1)} %convert_element_type.39.recv_ref, s32[256]{0:T(256)S(1)} %reshape.82.meta_ref, bf16[4,64,128,128]{3,2,1,0:T(8,128)(2,1)} %get-tuple-element.9.raw_ref, bf16[8,128,128]{2,1,0:T(8,128)(2,1)S(1)} %copy-done.5, ...), custom_call_target="tpu_custom_call" | custom-call | tf_op jit(solution)/shard_map/cross/pallas_call | solution.py:288
  127.0 0.0 copy-start.2
  127.0 53.8 %all_to_all.5.tiles_ref = bf16[64,128,128]{2,1,0:T(8,128)(2,1)S(1)} all-to-all(bf16[64,128,128]{2,1,0:T(8,128)(2,1)} %cross.1), channel_id=1, replica_groups=mesh['chan'=8,'tile'=4] {'chan'}, dimensions={0} | all-to-all | bytes 4194304 | tf_op jit(solution)/shard_map/all_to_all | solution.py:367
  180.8 0.0 copy-done.2
  180.8 4.0 %finish.1 = f32[512,2048]{1,0:T(8,128)} custom-call(s32[64]{0:T(128)S(1)} %reshape.77.slot_ref, s32[64]{0:T(128)S(1)} %reshape.78.kind_ref, bf16[64,128,128]{2,1,0:T(8,128)(2,1)S(1)} %all_to_all.5.tiles_ref, bf16[8,128,128]{2,1,0:T(8,128)(2,1)S(1)} %copy-done.5, bf16[512,2048]{1,0:T(8,128)(2,1)S(1)} %bitcast.14, f32[512,2048]{1,0:T(8,128)S(1)} %copy-done.2), custom_call_target="tpu_custom_call" | custom-call | tf_op jit(solution)/shard_map/finish/pallas_call | solution.py:317
  (10 shorter events, 0.2 us)
Async XLA Ops:
  3.0 1.6 copy-start
  4.6 2.3 %copy-start.6 = (f32[1,2048]{1,0:T(1,128)S(1)}, f32[1,2048]{1,0:T(1,128)}, u32[]{:S(2)}) copy-start(f32[1,2048]{1,0:T(1,128)} %param.8) | copy-start | bytes 24580
  4.6 2.3 %copy-start.7 = (s32[1,2048]{1,0:T(1,128)S(1)}, s32[1,2048]{1,0:T(1,128)}, u32[]{:S(2)}) copy-start(s32[1,2048]{1,0:T(1,128)} %param.9) | copy-start | bytes 24580
  4.6 2.8 %copy-start.1 = (bf16[1,512,2048]{2,1,0:T(8,128)(2,1)S(1)}, bf16[1,512,2048]{2,1,0:T(8,128)(2,1)}, u32[]{:S(2)}) copy-start(bf16[1,512,2048]{2,1,0:T(8,128)(2,1)} %param.7) | copy-start | bytes 6291460
  5.6 1.3 copy-start.3
  7.4 1.6 copy-start.4
  9.0 85.7 %copy-start.5 = (bf16[8,128,128]{2,1,0:T(8,128)(2,1)S(1)}, bf16[8,128,128]{2,1,0:T(8,128)(2,1)}, u32[]{:S(2)}) copy-start(bf16[8,128,128]{2,1,0:T(8,128)(2,1)} %recoup_ref.3) | copy-start | bytes 786436
  127.0 53.8 %copy-start.2 = (f32[512,2048]{1,0:T(8,128)S(1)}, f32[512,2048]{1,0:T(8,128)}, u32[]{:S(2)}) copy-start(f32[512,2048]{1,0:T(8,128)} %get-tuple-element.10.ladder_ref) | copy-start | bytes 12582916

commit v4 on v2

--- a/solution.py
+++ b/solution.py
@@ -253,11 +253,11 @@
         gamma_s[rows, cols] = both[tile:]
 
     def some(n, carry):
-        for u in range(4):
-            place(n * 4 + u)
-        return carry
-
-    lax.fori_loop(0, raw_ref.shape[0] * per_block // 4, some, 0)
+        for u in range(16):
+            place(n * 16 + u)
+        return carry
+
+    lax.fori_loop(0, raw_ref.shape[0] * per_block // 16, some, 0)
 
     own_rows = pl.ds(first, row_count)
     me = first // row_count

time: 189 us -> 179 us (0.947)
  Pallas kernels: 126 us -> 117 us
    pallas_call x1, Pallas kernels: 39.1 us -> 29.9 us  [cross_product(): pl.pallas_call(functools.partial(cross_kernel, width // tile, 256, row_co...]
where the time goes in v4:
time: 179 us
  Pallas kernels  117 us (65%)
  blocking collectives  52.8 us (29%)
  local copies, waits for them, and re-layouts  6.89 us (4%)
  other arithmetic  2.23 us (1%)
    pallas_call x1, Pallas kernels, exchange(): pl.pallas_call(functools.partial(exchange_kernel, n_chan, 256, count // n...  82.1 us
    all_to_all x1, blocking collectives, on_device(): lax.all_to_all(sym_tiles, 'chan', split_axis=0, concat_axis=0, tiled=True)  52.8 us
    pallas_call x1, Pallas kernels, cross_product(): pl.pallas_call(functools.partial(cross_kernel, width // tile, 256, row_co...  29.9 us
    unnamed x16, local copies, waits for them, and re-layouts  4.52 us
    pallas_call x1, Pallas kernels, finish(): pl.pallas_call(functools.partial(back_kernel, width // tile, 1.0 / math.s...  4.04 us

profile of v4, /device:TPU:0, one launch (start us, length us, event | category | flops | bytes accessed | tf_op | source)
XLA Modules:
  0.0 179.2 jit_solution(9355331442568596786)
XLA Ops:
  0.0 0.5 iota_multiply_fusion
  0.5 0.8 reshape.77.slot_ref
  1.3 0.8 reshape.78.kind_ref
  2.1 0.1 select_reduce_fusion
  2.2 0.7 convert_element_type.36
  2.9 0.1 convert_element_type.37
  3.0 0.0 copy-start
  3.0 1.6 copy-done
  4.6 0.0 copy-start.6
  4.6 0.0 copy-start.7
  4.6 0.0 copy-start.1
  4.6 1.0 sort_tiles.1.sorted_ref
  5.6 0.0 copy-start.3
  5.6 1.3 copy-done.3
  6.9 0.0 copy-done.6
  6.9 0.0 copy-done.7
  6.9 0.4 copy.11.xrow_ref
  7.3 0.1 fusion.info_ref
  7.4 0.0 copy-done.1
  7.4 0.0 copy-start.4
  7.4 1.6 copy-done.4
  9.0 0.0 copy-start.5
  9.0 82.1 %exchange.1 = (bf16[4,64,128,128]{3,2,1,0:T(8,128)(2,1)}, f32[8,4,8,128]{3,2,1,0:T(8,128)S(1)}, f32[512,2048]{1,0:T(8,128)}) custom-call(bf16[64,128,128]{2,1,0:T(8,128)(2,1)S(1)} %copy-done.4, bf16[512,2048]{1,0:T(8,128)(2,1)S(1)} %bitcast.13, f32[8,128]{1,0:T(8,128)S(1)} %fusion.info_ref, f32[2048,1]{1,0:T(8,128)S(1)} %copy.11.xrow_ref, ...), custom_call_target="tpu_custom_call" | custom-call | flops 8589934592 | bytes 67108864 | tf_op jit(solution)/shard_map/exchange/pallas_call | solution.py:195
  91.3 0.7 add_bitcast_fusion
  92.0 0.1 reshape.82.meta_ref
  92.1 0.1 dynamic-slice_convert_fusion
  92.2 0.1 convert_element_type.39.recv_ref
  92.3 0.1 copy.13
  92.4 0.0 copy-done.5
  92.4 29.9 %cross.1 = bf16[64,128,128]{2,1,0:T(8,128)(2,1)} custom-call(s32[1]{0:T(128)} %bitcast.where_ref, s32[256]{0:T(256)S(1)} %convert_element_type.39.recv_ref, s32[256]{0:T(256)S(1)} %reshape.82.meta_ref, bf16[4,64,128,128]{3,2,1,0:T(8,128)(2,1)} %get-tuple-element.9.raw_ref, bf16[8,128,128]{2,1,0:T(8,128)(2,1)S(1)} %copy-done.5, ...), custom_call_target="tpu_custom_call" | custom-call | tf_op jit(solution)/shard_map/cross/pallas_call | solution.py:282
  122.3 0.0 copy-start.2
  122.3 52.8 %all_to_all.5.tiles_ref = bf16[64,128,128]{2,1,0:T(8,128)(2,1)S(1)} all-to-all(bf16[64,128,128]{2,1,0:T(8,128)(2,1)} %cross.1), channel_id=1, replica_groups=mesh['chan'=8,'tile'=4] {'chan'}, dimensions={0} | all-to-all | bytes 4194304 | tf_op jit(solution)/shard_map/all_to_all | solution.py:361
  175.1 0.0 copy-done.2
  175.1 4.0 %finish.1 = f32[512,2048]{1,0:T(8,128)} custom-call(s32[64]{0:T(128)S(1)} %reshape.77.slot_ref, s32[64]{0:T(128)S(1)} %reshape.78.kind_ref, bf16[64,128,128]{2,1,0:T(8,128)(2,1)S(1)} %all_to_all.5.tiles_ref, bf16[8,128,128]{2,1,0:T(8,128)(2,1)S(1)} %copy-done.5, bf16[512,2048]{1,0:T(8,128)(2,1)S(1)} %bitcast.14, f32[512,2048]{1,0:T(8,128)S(1)} %copy-done.2), custom_call_target="tpu_custom_call" | custom-call | tf_op jit(solution)/shard_map/finish/pallas_call | solution.py:311
  (10 shorter events, 0.2 us)
Async XLA Ops:
  3.0 1.6 copy-start
  4.6 2.3 %copy-start.6 = (f32[1,2048]{1,0:T(1,128)S(1)}, f32[1,2048]{1,0:T(1,128)}, u32[]{:S(2)}) copy-start(f32[1,2048]{1,0:T(1,128)} %param.8) | copy-start | bytes 24580
  4.6 2.3 %copy-start.7 = (s32[1,2048]{1,0:T(1,128)S(1)}, s32[1,2048]{1,0:T(1,128)}, u32[]{:S(2)}) copy-start(s32[1,2048]{1,0:T(1,128)} %param.9) | copy-start | bytes 24580
  4.6 2.8 %copy-start.1 = (bf16[1,512,2048]{2,1,0:T(8,128)(2,1)S(1)}, bf16[1,512,2048]{2,1,0:T(8,128)(2,1)}, u32[]{:S(2)}) copy-start(bf16[1,512,2048]{2,1,0:T(8,128)(2,1)} %param.7) | copy-start | bytes 6291460
  5.6 1.3 copy-start.3
  7.4 1.6 copy-start.4
  9.0 83.4 %copy-start.5 = (bf16[8,128,128]{2,1,0:T(8,128)(2,1)S(1)}, bf16[8,128,128]{2,1,0:T(8,128)(2,1)}, u32[]{:S(2)}) copy-start(bf16[8,128,128]{2,1,0:T(8,128)(2,1)} %recoup_ref.3) | copy-start | bytes 786436
  122.3 52.8 %copy-start.2 = (f32[512,2048]{1,0:T(8,128)S(1)}, f32[512,2048]{1,0:T(8,128)}, u32[]{:S(2)}) copy-start(f32[512,2048]{1,0:T(8,128)} %get-tuple-element.10.ladder_ref) | copy-start | bytes 12582916
